TPU v7x, 32 devices: a whole 2x2x4 slice. The times are simulated.
32 devices in a mesh: grp: 2 (over y), ctx: 4 (over x, core), head: 4 (over z).
Axes of the slice: x: 2, y: 2, z: 4, core: 2. Of those that a mesh axis runs over, the one named last changes fastest.
Arguments:
- query_codes: bfloat16 [8192, 2048], P(('grp', 'ctx', 'head')), parts along dimension 0, may hold values from -0.5 to 2.5
- key_codes: bfloat16 [8192, 2048], P(('grp', 'ctx', 'head')), parts along dimension 0, may hold values from -0.5 to 2.5
- value_codes: bfloat16 [8192, 4096], P(('grp', 'ctx', 'head')), parts along dimension 0, may hold values from -6 to 6
- block_scales: float32 [64, 3, 8], P(('grp', 'ctx', 'head')), parts along dimension 0, may hold values from 0.25 to 2
- fault_tensor: int32 [64, 8], P(('grp', 'ctx', 'head')), parts along dimension 0, may hold values from 0 to 2
- fault_offset: int32 [64, 8], P(('grp', 'ctx', 'head')), parts along dimension 0, may hold values from 0 to 65535
- fault_bit: int32 [64, 8], P(('grp', 'ctx', 'head')), parts along dimension 0, may hold values from 0 to 3
- input_gate: bfloat16 [8192, 8], P(('grp', 'ctx', 'head')), parts along dimension 0, may hold values from -10 to 104
- forget_gate: bfloat16 [8192, 8], P(('grp', 'ctx', 'head')), parts along dimension 0, may hold values from 0.5 to 15
Outputs:
- hidden_states: bfloat16 [8192, 4096], P(('grp', 'ctx', 'head')), parts along dimension 0
There are 2 independent parts, one for each index of `grp`. A program takes and returns all parts, laid end to end along the dimension named above; each array names one. Nothing has to cross between parts.
All inputs are finite; a program needn't handle non-finite values.
Results may differ from a plain program's by a relative error of at most 0.0057.
Values may be sent and summed in bfloat16 or wider, within the bound.
A program may use at most 128 MiB of HBM per device.

v0:
```python
import math

import jax
import jax.numpy as jnp
from jax import lax
from jax.sharding import PartitionSpec as P

DK = 256
DV = 512
CH = 256
BLK = 128


NEG_FILL = -1e30


def entering(x, axis, combine, identity):
    peers, mine = (lax.axis_size(axis), lax.axis_index(axis))
    everything = jax.tree.map(lambda part: lax.all_gather(part, axis), x)
    start = jax.tree.map(
        lambda part, zero: jnp.broadcast_to(jnp.asarray(zero, part.dtype), part.shape), x, identity
    )

    def hop(k, before):
        reached = k < mine
        new = combine(before, jax.tree.map(lambda part: part[k], everything))
        return jax.tree.map(lambda a, b: jnp.where(reached, a, b), new, before)

    return lax.fori_loop(0, peers, hop, start)


def dequant(codes, scales, tensor_id, fault_tensor, fault_offset, fault_bit, width):
    rows = codes.shape[0]
    blocks = rows // BLK
    heads = scales.shape[2]
    shaped = codes.reshape(blocks, BLK, heads, width).astype(jnp.float32)
    block_factor = scales[:, tensor_id, :]
    struck = fault_tensor == tensor_id
    token_hit = fault_offset // DV
    column_hit = fault_offset % DV % width
    token_line = jnp.arange(BLK, dtype=jnp.int32)
    column_line = jnp.arange(width, dtype=jnp.int32)
    marked = (
        (token_line[None, :, None, None] == token_hit[:, None, :, None])
        & (column_line[None, None, None, :] == column_hit[:, None, :, None])
        & struck[:, None, :, None]
    )
    flipped = -jnp.exp2(fault_bit.astype(jnp.float32))
    factor = jnp.where(marked, flipped[:, None, :, None], jnp.ones_like(shaped))
    result = shaped * block_factor[:, None, :, None] * factor
    return result.reshape(rows, heads, width).astype(jnp.bfloat16)


def identity_state(groups):
    return (
        jnp.zeros((groups, DK, DV), jnp.float32),
        jnp.zeros((groups, DK), jnp.float32),
        jnp.full((groups,), NEG_FILL, jnp.float32),
        jnp.zeros((groups,), jnp.float32),
    )


def combine(earlier, following):
    peak = jnp.maximum(earlier[2] + following[3], following[2])
    first = jnp.exp(earlier[2] + following[3] - peak)
    second = jnp.exp(following[2] - peak)
    matrix = earlier[0] * first[..., None, None] + following[0] * second[..., None, None]
    normer = earlier[1] * first[..., None] + following[1] * second[..., None]
    return (matrix, normer, peak, earlier[3] + following[3])


def span_terms(lookup_vectors, values, gate_in, log_forget):
    running = jnp.cumsum(log_forget, axis=1)
    total = running[:, -1]
    exponent = total[:, None] - running + gate_in
    peak = jnp.max(exponent, axis=1)
    weights = jnp.exp(exponent - peak[:, None])
    weighted = (lookup_vectors.astype(jnp.float32) * weights[..., None]).astype(jnp.bfloat16)
    matrix = jnp.einsum("csgk,csgv->cgkv", weighted, values, preferred_element_type=jnp.float32)
    normer = jnp.sum(weighted.astype(jnp.float32), axis=1)
    return (matrix, normer, peak, total)


def prefix_states(states, start):

    def advance(carried, element):
        return (combine(carried, element), carried)

    return lax.scan(advance, start, states)


def span_outputs(queries, lookup_vectors, values, gate_in, log_forget, before):
    size = queries.shape[1]
    factor = 1.0 / math.sqrt(DK)
    running = jnp.cumsum(log_forget, axis=1).transpose(0, 2, 1)
    gate_rows = gate_in.transpose(0, 2, 1)
    exponent = running[..., :, None] - running[..., None, :] + gate_rows[..., None, :]
    line = jnp.arange(size, dtype=jnp.int32)
    causal = line[:, None] >= line[None, :]
    exponent = jnp.where(causal, exponent, NEG_FILL)
    inter = running + before[2][..., None]
    row_peak = jnp.maximum(jnp.max(exponent, axis=-1), inter)
    decay = jnp.exp(exponent - row_peak[..., None])
    scores = (
        jnp.einsum("ctgk,csgk->cgts", queries, lookup_vectors, preferred_element_type=jnp.float32)
        * factor
    )
    product = decay * scores
    product_weights = product.astype(jnp.bfloat16)
    numerator = jnp.einsum(
        "cgts,csgv->ctgv", product_weights, values, preferred_element_type=jnp.float32
    )
    lift = jnp.exp(inter - row_peak)
    lifted = (queries.astype(jnp.float32) * (factor * lift).transpose(0, 2, 1)[..., None]).astype(
        jnp.bfloat16
    )
    start_matrix = before[0].astype(jnp.bfloat16)
    numerator = numerator + jnp.einsum(
        "ctgk,cgkv->ctgv", lifted, start_matrix, preferred_element_type=jnp.float32
    )
    denominator = jnp.sum(product, axis=-1) + jnp.einsum(
        "ctgk,cgk->cgt", lifted.astype(jnp.float32), before[1], precision=lax.Precision.HIGHEST
    )
    floor_value = jnp.maximum(jnp.abs(denominator), 1.0)
    return (numerator / floor_value.transpose(0, 2, 1)[..., None]).astype(jnp.bfloat16)


def in_spans(array, width):
    spans = array.shape[0] // CH
    if width == 0:
        return array.reshape(spans, CH, array.shape[1])
    return array.reshape(spans, CH, array.shape[1], width)


def body(
    query_codes,
    key_codes,
    value_codes,
    block_scales,
    fault_tensor,
    fault_offset,
    fault_bit,
    input_gate,
    forget_gate,
):
    queries = dequant(query_codes, block_scales, 0, fault_tensor, fault_offset, fault_bit, DK)
    lookup_vectors = dequant(key_codes, block_scales, 1, fault_tensor, fault_offset, fault_bit, DK)
    values = dequant(value_codes, block_scales, 2, fault_tensor, fault_offset, fault_bit, DV)
    tok_rows = queries.shape[0]
    got_q, got_k, got_v, got_i, got_f = (
        lax.all_to_all(queries, "head", split_axis=1, concat_axis=0, tiled=True),
        lax.all_to_all(lookup_vectors, "head", split_axis=1, concat_axis=0, tiled=True),
        lax.all_to_all(values, "head", split_axis=1, concat_axis=0, tiled=True),
        lax.all_to_all(input_gate, "head", split_axis=1, concat_axis=0, tiled=True),
        lax.all_to_all(forget_gate, "head", split_axis=1, concat_axis=0, tiled=True),
    )
    length = got_q.shape[0]
    groups = got_q.shape[1]
    span_q = in_spans(got_q, DK)
    span_k = in_spans(got_k, DK)
    span_v = in_spans(got_v, DV)
    gate_in = in_spans(got_i.astype(jnp.float32), 0)
    log_forget = in_spans(jax.nn.log_sigmoid(got_f.astype(jnp.float32)), 0)
    terms = span_terms(span_k, span_v, gate_in, log_forget)
    total, before_local = prefix_states(terms, identity_state(groups))
    incoming = entering(total, "ctx", combine, identity_state(groups))
    before = combine(incoming, before_local)
    hidden = span_outputs(span_q, span_k, span_v, gate_in, log_forget, before).reshape(
        length, groups, DV
    )
    hidden_rows = lax.all_to_all(hidden, "head", split_axis=0, concat_axis=1, tiled=True)
    return hidden_rows.reshape(tok_rows, -1)


def solution(mesh):
    placed = (
        P(("grp", "ctx", "head"), None),
        P(("grp", "ctx", "head"), None),
        P(("grp", "ctx", "head"), None),
        P(("grp", "ctx", "head"), None, None),
        P(("grp", "ctx", "head"), None),
        P(("grp", "ctx", "head"), None),
        P(("grp", "ctx", "head"), None),
        P(("grp", "ctx", "head"), None),
        P(("grp", "ctx", "head"), None),
    )
    return jax.shard_map(
        body, mesh=mesh, in_specs=placed, out_specs=P(("grp", "ctx", "head"), None), check_vma=False
    )
```

profile of v0, /device:TPU:2, one launch (start us, length us, event | category | flops | bytes accessed | tf_op | source)
XLA Modules:
  0.0 246.3 jit_solution(14191822384164090131)
XLA Ops:
  6.5 1.4 all_to_all.67
  7.9 4.9 %all-to-all-start.1 = ((bf16[256,4,2]{0,2,1:T(2,128)(2,1)}), bf16[256,4,2]{0,2,1:T(2,128)(2,1)S(1)}, u32[]{:S(2)}, u32[]{:S(2)}) async-start(bf16[256,4,2]{0,2,1:T(2,128)(2,1)} %all_to_all.67), calls=%async_computation.1 | async-start | bytes 8192 | tf_op jit(solution)/shard_map/all_to_all | solution.py:155
  13.5 0.7 slice_bitcast_fusion.1
  14.9 0.7 and_select_fusion
  16.0 1.3 all_to_all.69
  17.2 1.1 all-to-all-done.1
  18.4 4.0 %all-to-all-start.2 = ((bf16[256,4,2]{0,2,1:T(2,128)(2,1)}), bf16[256,4,2]{0,2,1:T(2,128)(2,1)S(1)}, u32[]{:S(2)}, u32[]{:S(2)}) async-start(bf16[256,4,2]{0,2,1:T(2,128)(2,1)} %all_to_all.69), calls=%async_computation.2 | async-start | bytes 8192 | tf_op jit(solution)/shard_map/all_to_all | solution.py:154
  22.4 1.5 convert_element_type.105
  24.1 4.3 %fusion.23 = (bf16[256,8,256]{2,0,1:T(8,128)(2,1)}, bf16[256,8,256]{2,0,1:T(8,128)(2,1)}) fusion(f32[32,8,8,256]{3,2,1,0:T(8,128)S(1)} %bitcast.234, f32[256,8]{0,1:T(8,128)S(1)} %get-tuple-element.445, f32[256,8]{0,1:T(8,128)S(1)} %get-tuple-element.442, pred[256,8]{0,1:T(8,128)(4,1)S(1)} %get-tuple-element.444, ...), kind=kLoop, calls=%fused_computation.48 | loop fusion | flops 5767168 | bytes 6326272 | tf_op jit(solution)/shard_map/convert_element_type | solution.py:51
  28.5 5.1 %all-to-all-start.3 = ((bf16[256,8,256]{2,0,1:T(8,128)(2,1)}), bf16[256,8,256]{2,0,1:T(8,128)(2,1)S(1)}, u32[]{:S(2)}, u32[]{:S(2)}) async-start(bf16[256,8,256]{2,0,1:T(8,128)(2,1)} %get-tuple-element.430), calls=%async_computation.3 | async-start | bytes 2097152 | tf_op jit(solution)/shard_map/all_to_all | solution.py:152
  33.6 4.0 %convert_element_type.102 = f32[256,4096]{1,0:T(8,128)} convert(bf16[256,4096]{1,0:T(8,128)(2,1)} %param.15) | non-fusion elementwise | flops 1048576 | bytes 6291456 | tf_op jit(solution)/shard_map/convert_element_type | solution.py:36
  37.9 4.8 %fusion.17 = bf16[256,8,512]{2,0,1:T(8,128)(2,1)} fusion(f32[32,8,8,512]{3,2,1,0:T(8,128)} %bitcast.230, f32[256,8]{0,1:T(8,128)S(1)} %get-tuple-element.445, f32[256,8]{0,1:T(8,128)S(1)} %get-tuple-element.446, pred[256,8]{0,1:T(8,128)(4,1)S(1)} %broadcast_bitcast_fusion.6, pred[2,8,512]{2,0,1:T(4,128)(4,1)S(1)} %iota_compare_fusion.1, ...), kind=kLoop, calls=%fused_computation.37 | loop fusion | flops 6291456 | bytes 6320128 | tf_op jit(solution)/shard_map/convert_element_type | solution.py:51
  42.7 15.5 %all-to-all-done.3 = bf16[256,8,256]{2,0,1:T(8,128)(2,1)S(1)} async-done(((bf16[256,8,256]{2,0,1:T(8,128)(2,1)}), bf16[256,8,256]{2,0,1:T(8,128)(2,1)S(1)}, u32[]{:S(2)}, u32[]{:S(2)}) %all-to-all-start.3) | async-done | bytes 1048608 | tf_op jit(solution)/shard_map/all_to_all | solution.py:152
  58.2 1.0 copy-done.1
  59.1 3.6 %all-to-all-start = ((bf16[256,8,512]{2,0,1:T(8,128)(2,1)}), bf16[256,8,512]{2,0,1:T(8,128)(2,1)S(1)}, u32[]{:S(2)}, u32[]{:S(2)}) async-start(bf16[256,8,512]{2,0,1:T(8,128)(2,1)} %fusion.17), calls=%async_computation | async-start | bytes 4194304 | tf_op jit(solution)/shard_map/all_to_all | solution.py:153
  62.9 2.4 reduce-window.6
  66.3 1.6 convert_reduce_fusion
  67.9 42.5 %all-to-all-done = bf16[256,8,512]{2,0,1:T(8,128)(2,1)S(1)} async-done(((bf16[256,8,512]{2,0,1:T(8,128)(2,1)}), bf16[256,8,512]{2,0,1:T(8,128)(2,1)S(1)}, u32[]{:S(2)}, u32[]{:S(2)}) %all-to-all-start) | async-done | bytes 2097184 | tf_op jit(solution)/shard_map/all_to_all | solution.py:153
  110.4 4.3 %fusion.32 = f32[4,2,256,512]{3,2,1,0:T(8,128)} fusion(bf16[4,256,2,512]{3,1,2,0:T(8,128)(2,1)S(1)} %bitcast.228, bf16[4,256,2,256]{3,1,2,0:T(8,128)(2,1)} %bitcast.232, f32[4,256,2]{1,2,0:T(2,128)S(1)} %subtract_exponential_fusion.4), kind=kOutput, calls=%fused_computation.63 | convolution fusion | flops 538443776 | bytes 7348224 | tf_op jit(solution)/shard_map/csgk,csgv->cgkv/dot_general | solution.py:79
  114.7 11.4 %while.45 = (s32[]{:T(128)}, f32[2,256,512]{2,1,0:T(8,128)S(1)}, f32[2,256]{1,0:T(2,128)S(1)}, f32[2]{0:T(128)S(1)}, f32[2]{0:T(128)S(1)}, /*index=5*/f32[4,2,25...) while((s32[]{:T(128)}, f32[2,256,512]{2,1,0:T(8,128)S(1)}, ...), condition=%wide.region_6.7_spmd.clone.clone, body=%wide.region_5.6_spmd.clone.sunk.clone | while | flops 1313299 | bytes 5253468 | solution.py:89
  114.7 1.1 bitcast_dynamic-update-slice_fusion.6
  115.8 1.6 fusion.63
  117.5 1.1 bitcast_dynamic-update-slice_fusion.6
  118.6 1.6 fusion.63
  120.4 1.1 bitcast_dynamic-update-slice_fusion.6
  121.5 1.6 fusion.63
  123.2 1.1 bitcast_dynamic-update-slice_fusion.6
  124.4 1.6 fusion.63
  126.1 1.0 copy-done
  127.1 4.3 %all-to-all-start.4 = ((bf16[256,8,256]{2,0,1:T(8,128)(2,1)}), bf16[256,8,256]{2,0,1:T(8,128)(2,1)}, u32[]{:S(2)}, u32[]{:S(2)}) async-start(bf16[256,8,256]{2,0,1:T(8,128)(2,1)} %get-tuple-element.431), calls=%async_computation.4 | async-start | bytes 2097152 | tf_op jit(solution)/shard_map/all_to_all | solution.py:151
  133.2 0.7 fusion.27
  133.9 6.1 %all-reduce.2 = (f32[8]{0:T(128)S(1)}, f32[8]{0:T(128)S(1)}) all-reduce(f32[8]{0:T(128)S(1)} %dynamic-update-slice, f32[8]{0:T(128)S(1)} %dynamic-update-slice.1), channel_id=2, replica_groups=mesh['grp'=2,'ctx'=4,'head'=4] {'ctx'}, use_global_device_ids=true, to_apply=%add | all-reduce | flops 16 | bytes 128
  140.2 5.3 %all-gather.4 = f32[4,2,256]{2,1,0:T(2,128)S(1)} all-gather(f32[1,2,256]{2,1,0:T(2,128)S(1)} %bitcast.241), channel_id=5, replica_groups=mesh['grp'=2,'ctx'=4,'head'=4] {'ctx'}, dimensions={0}, use_global_device_ids=true | all-gather | bytes 10240 | tf_op jit(solution)/shard_map/all_gather | solution.py:19
  145.6 14.3 %all-gather.7.cloned.1.call-done = f32[8,256,512]{2,1,0:T(8,128)} async-done(((f32[2,256,512]{2,1,0:T(8,128)}), f32[8,256,512]{2,1,0:T(8,128)}) %all-gather.7.cloned.1.call-update) | async-done | bytes 4194320 | tf_op jit(solution)/shard_map/all_gather | solution.py:19
  159.9 7.8 %while.46 = (s32[]{:T(128)}, f32[2,256,512]{2,1,0:T(8,128)S(1)}, f32[2,256]{1,0:T(2,128)S(1)}, f32[2]{0:T(128)S(1)}, s32[]{:T(128)}, /*index=5*/f32[4,2]{1,0:T(4...) while((s32[]{:T(128)}, f32[2,256,512]{2,1,0:T(8,128)S(1)}, ...), condition=%wide.region_8.9_spmd.clone.clone, body=%wide.region_7.8_spmd.clone.sunk.clone | while | flops 1313298 | bytes 3152117 | solution.py:29
  159.9 1.8 fusion.66
  161.8 1.8 fusion.66
  163.8 1.8 fusion.66
  165.7 1.8 fusion.66
  167.8 2.4 fusion.47
  170.2 0.8 fusion.30
  171.0 2.6 %fusion.33 = f32[4,2,1,256]{3,2,1,0:T(1,128)S(1)} fusion(bf16[4,256,2,256]{3,1,2,0:T(8,128)(2,1)} %bitcast.29, f32[4,256,2]{1,2,0:T(2,128)S(1)} %get-tuple-element.428, f32[4,2,256,1]{2,1,0,3:T(2,128)S(1)} %add_bitcast_fusion), kind=kOutput, calls=%fused_computation.64 | convolution fusion | flops 7864320 | bytes 1073152 | tf_op jit(solution)/shard_map/ctgk,cgk->cgt/dot_general | solution.py:121
  173.7 2.8 %fusion.18 = bf16[4,256,2,512]{3,1,2,0:T(8,128)(2,1)S(1)} fusion(f32[4,2,512,256]{2,3,1,0:T(8,128)S(1)} %fusion.30, f32[4,2,256,512]{3,2,1,0:T(8,128)S(1)} %copy-done.3, f32[4,256,2]{1,2,0:T(2,128)S(1)} %fusion.38, f32[4,2]{1,0:T(4,128)S(1)} %subtract_exponential_fusion.5, f32[4,2]{1,0:T(4,128)S(1)} %get-tuple-element.420, ...), kind=kOutput, calls=%fused_computation.39 | convolution fusion | flops 545783808 | bytes 12599360 | tf_op jit(solution)/shard_map/ctgk,cgkv->ctgv/dot_general | solution.py:118
  176.8 2.2 copy.75
  178.9 53.2 %all_to_all.86 = bf16[1024,2,512]{2,1,0:T(2,128)(2,1)S(1)} all-to-all(bf16[1024,2,512]{2,1,0:T(2,128)(2,1)S(1)} %copy.75), channel_id=1, replica_groups=mesh['grp'=2,'ctx'=4,'head'=4] {'head'}, dimensions={0} | all-to-all | bytes 4194304 | tf_op jit(solution)/shard_map/all_to_all | solution.py:171
  232.2 1.7 copy.76
  233.8 2.8 %copy.77 = bf16[256,4,2,512]{0,3,2,1:T(8,128)(2,1)S(1)} copy(bf16[256,4,2,512]{3,0,1,2:T(8,128)(2,1)} %bitcast.237) | data formatting | bytes 4194304 | tf_op jit(solution)/shard_map/all_to_all | solution.py:171
  236.6 2.9 %copy.78 = bf16[256,4096]{1,0:T(8,128)(2,1)} copy(bf16[256,4096]{0,1:T(8,128)(2,1)S(1)} %bitcast.238) | data formatting | bytes 4194304 | tf_op jit(solution)/shard_map/reshape | solution.py:172
  (106 shorter events, 6.3 us)
Async XLA Ops:
  6.5 17.4 %copy-start.2 = (bf16[256,2048]{1,0:T(8,128)(2,1)S(1)}, bf16[256,2048]{1,0:T(8,128)(2,1)}, u32[]{:S(2)}) copy-start(bf16[256,2048]{1,0:T(8,128)(2,1)} %param.13) | copy-start | bytes 3145732
  7.9 10.4 %all-to-all-start.1 = ((bf16[256,4,2]{0,2,1:T(2,128)(2,1)}), bf16[256,4,2]{0,2,1:T(2,128)(2,1)S(1)}, u32[]{:S(2)}, u32[]{:S(2)}) async-start(bf16[256,4,2]{0,2,1:T(2,128)(2,1)} %all_to_all.67), calls=%async_computation.1 | async-start | bytes 8192 | tf_op jit(solution)/shard_map/all_to_all | solution.py:155
  18.4 10.1 %all-to-all-start.2 = ((bf16[256,4,2]{0,2,1:T(2,128)(2,1)}), bf16[256,4,2]{0,2,1:T(2,128)(2,1)S(1)}, u32[]{:S(2)}, u32[]{:S(2)}) async-start(bf16[256,4,2]{0,2,1:T(2,128)(2,1)} %all_to_all.69), calls=%async_computation.2 | async-start | bytes 8192 | tf_op jit(solution)/shard_map/all_to_all | solution.py:154
  28.5 29.7 %all-to-all-start.3 = ((bf16[256,8,256]{2,0,1:T(8,128)(2,1)}), bf16[256,8,256]{2,0,1:T(8,128)(2,1)S(1)}, u32[]{:S(2)}, u32[]{:S(2)}) async-start(bf16[256,8,256]{2,0,1:T(8,128)(2,1)} %get-tuple-element.430), calls=%async_computation.3 | async-start | bytes 2097152 | tf_op jit(solution)/shard_map/all_to_all | solution.py:152
  58.2 1.0 copy-start.1
  59.1 51.3 %all-to-all-start = ((bf16[256,8,512]{2,0,1:T(8,128)(2,1)}), bf16[256,8,512]{2,0,1:T(8,128)(2,1)S(1)}, u32[]{:S(2)}, u32[]{:S(2)}) async-start(bf16[256,8,512]{2,0,1:T(8,128)(2,1)} %fusion.17), calls=%async_computation | async-start | bytes 4194304 | tf_op jit(solution)/shard_map/all_to_all | solution.py:153
  62.7 97.1 %all-gather.7.cloned.1.call-start = ((), (), s32[]{:S(2)}) async-start(), calls=%async_computation.6 | async-start | bytes 5242880 | tf_op jit(solution)/shard_map/all_gather | solution.py:19
  126.1 1.0 copy-start
  126.1 5.3 %copy-start.4 = (u32[32]{0:T(128)S(1)}, u32[32]{0:T(128)}, u32[]{:S(2)}) copy-start(u32[32]{0:T(128)} %constant.143) | copy-start | bytes 388
  127.1 40.6 %all-to-all-start.4 = ((bf16[256,8,256]{2,0,1:T(8,128)(2,1)}), bf16[256,8,256]{2,0,1:T(8,128)(2,1)}, u32[]{:S(2)}, u32[]{:S(2)}) async-start(bf16[256,8,256]{2,0,1:T(8,128)(2,1)} %get-tuple-element.431), calls=%async_computation.4 | async-start | bytes 2097152 | tf_op jit(solution)/shard_map/all_to_all | solution.py:151
  170.2 3.5 %copy-start.3 = (f32[4,2,256,512]{3,2,1,0:T(8,128)S(1)}, f32[4,2,256,512]{3,2,1,0:T(8,128)}, u32[]{:S(2)}) copy-start(f32[4,2,256,512]{3,2,1,0:T(8,128)} %get-tuple-element.243) | copy-start | bytes 12582916
Sparse Core Ops, SparseCore 0:
  127.2 32.5 all-gather.6
where the time goes:
time: 250 us; the launch traced here: 246 us
  waiting for transfers between devices  73.4 us (29%)
  blocking collectives  64.7 us (26%)
  other arithmetic  41.4 us (17%)
  starting transfers between devices  21.9 us (9%)
  local copies, waits for them, and re-layouts  17.6 us (7%)
  between operations  14.4 us (6%)
  matrix products  12.9 us (5%)
    all_to_all x1, blocking collectives, body(): lax.all_to_all(hidden, 'head', split_axis=0, concat_axis=1, tiled=True)  53.2 us
    all_to_all x1, waiting for transfers between devices, body(): lax.all_to_all(values, 'head', split_axis=1, concat_axis=0, tiled=True)  42.5 us
    all_to_all x1, waiting for transfers between devices, body(): lax.all_to_all(lookup_vectors, 'head', split_axis=1, concat_axis=0, tiled...  15.5 us
    all_gather x1, waiting for transfers between devices, entering(): everything = jax.tree.map(lambda part: lax.all_gather(part, axis), x)  14.3 us
    convert_element_type x2, other arithmetic, dequant(): return result.reshape(rows, heads, width).astype(jnp.bfloat16)  9.17 us
    select_n x12, other arithmetic, hop(): return jax.tree.map(lambda a, b: jnp.where(reached, a, b), new, before)  7.68 us
    add x4, other arithmetic, combine(): earlier[0] * first[..., None, None] + following[0] * second[..., None, None]  6.24 us
    unnamed x1, blocking collectives  6.13 us
  transfers between devices with their start and end apart: 6, of which 4 were waited for; matrix products, arithmetic and copies ran while one was open for 14% of the time, Pallas kernels for 0%

commit v1 on v0

v1 whole, which is shorter than its diff:
```python
import functools
import math

import jax
import jax.numpy as jnp
from jax import lax
from jax.experimental import pallas as pl
from jax.experimental.pallas import tpu as pltpu
from jax.sharding import PartitionSpec as P

BLK = 128
PIECES = 2
NEG_FILL = -1e30
MESH = pl.DeviceIdType.MESH
F32 = jnp.float32
BF16 = jnp.bfloat16


def kernel(
    sizes,
    q_ref,
    k_ref,
    v_ref,
    scale_ref,
    ft_ref,
    fo_ref,
    fb_ref,
    ig_ref,
    fg_ref,
    out_ref,
    qd,
    kd,
    vd,
    wk,
    num,
    lifted,
    up_buf,
    tot_buf,
    r_buf,
    rs_buf,
    bcol,
    wcol,
    brow,
    grow,
    peak_l,
    den_l,
    fin,
    own_h,
    up_h,
    tot_h,
    r_h,
    rs_h,
    wts,
    up_s,
    up_r,
    dn_s,
    r_r,
    cx_s,
    hs,
):
    heads, dk, dv, nc, nz = sizes
    rows = q_ref.shape[0]
    pw = dv // PIECES
    pieces = heads * PIECES
    factor = 1.0 / math.sqrt(dk)
    g, c, z = lax.axis_index("grp"), lax.axis_index("ctx"), lax.axis_index("head")
    last = nz - 1
    has_up, has_down = z < last, z > 0
    at_end = z == last
    gives_row, has_row = at_end & (c < nc - 1), c > 0
    above = (g, c, jnp.minimum(z + 1, last))
    below = (g, c, jnp.maximum(z - 1, 0))
    after = (g, jnp.minimum(c + 1, nc - 1), z)
    earlier = (g, jnp.maximum(c - 1, 0), z)

    barrier = pltpu.get_barrier_semaphore()
    greet = ((has_up, above), (has_down, below), (gives_row, after), (at_end & has_row, earlier))
    for there, who in greet:

        @pl.when(there)
        def _(who=who):
            pl.semaphore_signal(barrier, inc=1, device_id=who, device_id_type=MESH)

    def remote(src, dst, ssem, rsem, who):
        return pltpu.make_async_remote_copy(
            src_ref=src, dst_ref=dst, send_sem=ssem, recv_sem=rsem,
            device_id=who, device_id_type=MESH,
        )

    def up_copy(i):
        return remote(tot_buf.at[i], up_buf.at[i], up_s.at[i], up_r.at[i], above)

    def down_copy(i):
        return remote(r_buf.at[i], r_buf.at[i], dn_s.at[i], r_r.at[i], below)

    def row_copy(i):
        return remote(rs_buf.at[i], r_buf.at[i], cx_s.at[i], r_r.at[i], after)

    up_head = remote(tot_h, up_h, hs.at[0], hs.at[1], above)
    down_head = remote(r_h, r_h, hs.at[2], hs.at[3], below)
    row_head = remote(rs_h, r_h, hs.at[4], hs.at[3], after)

    token = lax.broadcasted_iota(jnp.int32, (BLK, 1), 0)

    def dequant(codes, e, h, width, kept):
        col = lax.broadcasted_iota(jnp.int32, (BLK, width), 1)
        start = pl.multiple_of(h * width, width)
        for b in range(rows // BLK):
            place = (pl.ds(b * BLK, BLK), pl.ds(start, width))
            off = fo_ref[b, h]
            bit = fb_ref[b, h]
            flip = jnp.where(bit >= 1, -2.0, -1.0)
            flip = flip * jnp.where(bit >= 2, 2.0, 1.0) * jnp.where(bit >= 3, 2.0, 1.0)
            flip = jnp.where(ft_ref[b, h] == e, flip, 1.0)
            hit = lax.rem(lax.rem(off, dv), width)
            line = jnp.where(token == lax.div(off, dv), hit, -1)
            scale = scale_ref[b, e, h]
            times = jnp.where(col == line, scale * flip, scale)
            kept[place] = (codes[place].astype(F32) * times).astype(BF16)
        return start

    lane = lax.broadcasted_iota(jnp.int32, (rows, heads), 1)

    def column(ref, h):
        return jnp.sum(jnp.where(lane == h, ref[...], 0.0), axis=1, keepdims=True)

    line_t = lax.broadcasted_iota(jnp.int32, (rows, rows), 0)
    line_s = lax.broadcasted_iota(jnp.int32, (rows, rows), 1)
    forget = fg_ref[...].astype(F32)
    logf = -(jnp.maximum(-forget, 0.0) + jnp.log1p(jnp.exp(-jnp.abs(forget))))
    gate = ig_ref[...].astype(F32)
    running = jnp.dot(
        (line_t >= line_s).astype(F32), logf,
        preferred_element_type=F32, precision=lax.Precision.HIGHEST,
    )
    bcol[...] = running
    brow[...] = running.T
    grow[...] = gate.T
    exponent = running[rows - 1 : rows, :] - running + gate
    wcol[...] = jnp.exp(exponent - jnp.max(exponent, axis=0, keepdims=True))
    total = brow[:, rows - 1 : rows]
    peak = jnp.max(total - brow[...] + grow[...], axis=1, keepdims=True)
    own_h[:, dk : 2 * dk] = jnp.broadcast_to(peak, (heads, dk))
    own_h[:, 2 * dk :] = jnp.broadcast_to(total, (heads, dk))

    def keys(h, carry):
        start = dequant(k_ref, 1, h, dk, kd)
        place = (slice(None), pl.ds(start, dk))
        weighted = (kd[place].astype(F32) * column(wcol, h)).astype(BF16)
        wk[place] = weighted
        own_h[pl.ds(h, 1), pl.ds(0, dk)] = jnp.sum(weighted.astype(F32), axis=0, keepdims=True)
        return carry

    lax.fori_loop(0, heads, keys, 0)

    def empty_header(ref):
        ref[:, 0:dk] = jnp.zeros((heads, dk), F32)
        ref[:, dk : 2 * dk] = jnp.full((heads, dk), NEG_FILL, F32)
        ref[:, 2 * dk :] = jnp.zeros((heads, dk), F32)

    @pl.when(z == 0)
    def _():
        empty_header(up_h)
        up_buf[...] = jnp.zeros_like(up_buf)

    @pl.when(c == 0)
    def _():
        empty_header(r_h)
        r_buf[...] = jnp.zeros_like(r_buf)

    def join(first, later, dst, at):
        m1, m2, f2 = first[:, dk : 2 * dk], later[:, dk : 2 * dk], later[:, 2 * dk :]
        m = jnp.maximum(m1 + f2, m2)
        w1, w2 = jnp.exp(m1 + f2 - m), jnp.exp(m2 - m)
        wts[at] = w1
        wts[at + 1] = w2
        dst[:, 0:dk] = w1 * first[:, 0:dk] + w2 * later[:, 0:dk]
        dst[:, dk : 2 * dk] = m
        dst[:, 2 * dk :] = first[:, 2 * dk :] + f2

    greeted = sum(there.astype(jnp.int32) for there, _ in greet)
    pl.semaphore_wait(barrier, greeted)

    @pl.when(has_down)
    def _():
        up_head.wait_recv()

    join(up_h, own_h, tot_h, 0)

    @pl.when(has_up)
    def _():
        up_head.start()

    def weight(at, h):
        return wts[at, pl.ds(h, 1), :][:, 0:pw]

    def local(h):
        start = dequant(q_ref, 0, h, dk, qd)
        place = (slice(None), pl.ds(start, dk))
        scores = lax.dot_general(
            qd[place], kd[place], (((1,), (1,)), ((), ())), preferred_element_type=F32
        ) * factor
        gaps = column(bcol, h) - brow[pl.ds(h, 1), :] + grow[pl.ds(h, 1), :]
        gaps = jnp.where(line_t >= line_s, gaps, NEG_FILL)
        top = jnp.max(gaps, axis=1, keepdims=True)
        product = jnp.exp(gaps - top) * scores
        peak_l[h] = jnp.broadcast_to(top, (rows, BLK))
        den_l[h] = jnp.broadcast_to(jnp.sum(product, axis=1, keepdims=True), (rows, BLK))
        wide = (slice(None), pl.ds(pl.multiple_of(h * dv, dv), dv))
        num[wide] = jnp.dot(product.astype(BF16), vd[wide], preferred_element_type=F32)

    def upward(i):
        h = lax.div(i, PIECES)

        @pl.when(lax.rem(i, PIECES) == 0)
        def _():
            dequant(v_ref, 2, h, dv, vd)

        piece = pl.ds(pl.multiple_of(i * pw, pw), pw)
        state = lax.dot_general(
            wk[:, pl.ds(pl.multiple_of(h * dk, dk), dk)], vd[:, piece],
            (((0,), (0,)), ((), ())), preferred_element_type=F32,
        )

        @pl.when(has_down)
        def _():
            up_copy(i).wait_recv()

        tot_buf[i] = (weight(0, h) * up_buf[i].astype(F32) + weight(1, h) * state).astype(BF16)

        @pl.when(has_up)
        def _():
            up_copy(i).start()

        @pl.when(lax.rem(i, PIECES) == 0)
        def _():
            local(h)

    def header_row():
        @pl.when(has_row)
        def _():
            down_head.wait_recv()

        @pl.when(has_row & has_down)
        def _():
            down_head.start()

        @pl.when(gives_row)
        def _():
            join(r_h, tot_h, rs_h, 2)
            row_head.start()

        join(r_h, up_h, own_h, 4)

    def finish(j):
        h = lax.div(j, PIECES)

        @pl.when(j == 0)
        def _():
            header_row()

        @pl.when(has_row)
        def _():
            down_copy(j).wait_recv()

        @pl.when(has_row & has_down)
        def _():
            down_copy(j).start()

        arrived = r_buf[j].astype(F32)

        @pl.when(gives_row)
        def _():
            rs_buf[j] = (weight(2, h) * arrived + weight(3, h) * tot_buf[j].astype(F32)).astype(BF16)
            row_copy(j).start()

        @pl.when(lax.rem(j, PIECES) == 0)
        def _():
            place = (slice(None), pl.ds(pl.multiple_of(h * dk, dk), dk))
            header = own_h[pl.ds(h, 1), :]
            norm, m = header[:, 0:dk], header[:, dk : dk + BLK]
            inter = column(bcol, h) + m
            top = jnp.maximum(peak_l[h], inter)
            shrink = jnp.exp(peak_l[h] - top)
            lift = jnp.exp(inter - top) * factor
            raised = (qd[place].astype(F32) * lift[:, 0:1]).astype(BF16)
            lifted[...] = raised
            den = shrink * den_l[h] + jnp.sum(raised.astype(F32) * norm, axis=1, keepdims=True)
            fin[0] = shrink
            fin[1] = 1.0 / jnp.maximum(jnp.abs(den), 1.0)

        piece = pl.ds(pl.multiple_of(j * pw, pw), pw)
        begin = (weight(4, h) * arrived + weight(5, h) * up_buf[j].astype(F32)).astype(BF16)
        above_line = num[:, piece] * fin[0][:, 0:1] + jnp.dot(
            lifted[...], begin, preferred_element_type=F32
        )
        out_ref[:, piece] = (above_line * fin[1][:, 0:1]).astype(BF16)

    skew = 2 * (last - z) + c

    def step(t, carry):
        @pl.when(t < pieces)
        def _():
            upward(t)

        @pl.when(t >= skew)
        def _():
            finish(t - skew)

        return carry

    lax.fori_loop(0, pieces + skew, step, 0)

    @pl.when(has_up)
    def _():
        up_head.wait_send()

    @pl.when(has_row & has_down)
    def _():
        down_head.wait_send()

    @pl.when(gives_row)
    def _():
        row_head.wait_send()

    def drain(i, carry):
        @pl.when(has_up)
        def _():
            up_copy(i).wait_send()

        @pl.when(has_row & has_down)
        def _():
            down_copy(i).wait_send()

        @pl.when(gives_row)
        def _():
            row_copy(i).wait_send()

        return carry

    lax.fori_loop(0, pieces, drain, 0)


def body(nc, nz, *args):
    rows = args[0].shape[0]
    heads = args[3].shape[2]
    dk, dv = args[0].shape[1] // heads, args[2].shape[1] // heads
    pieces, pw = heads * PIECES, dv // PIECES
    vmem, smem = pl.BlockSpec(memory_space=pltpu.VMEM), pl.BlockSpec(memory_space=pltpu.SMEM)
    passed = pltpu.VMEM((pieces, dk, pw), BF16)
    header = pltpu.VMEM((heads, 3 * dk), F32)
    sems = pltpu.SemaphoreType.DMA((pieces,))
    return pl.pallas_call(
        functools.partial(kernel, (heads, dk, dv, nc, nz)),
        out_shape=jax.ShapeDtypeStruct((rows, heads * dv), BF16),
        in_specs=[vmem] * 3 + [smem] * 4 + [vmem] * 2,
        out_specs=vmem,
        scratch_shapes=[
            pltpu.VMEM((rows, heads * dk), BF16),
            pltpu.VMEM((rows, heads * dk), BF16),
            pltpu.VMEM((rows, heads * dv), BF16),
            pltpu.VMEM((rows, heads * dk), BF16),
            pltpu.VMEM((rows, heads * dv), F32),
            pltpu.VMEM((rows, dk), BF16),
            passed,
            passed,
            passed,
            passed,
            pltpu.VMEM((rows, heads), F32),
            pltpu.VMEM((rows, heads), F32),
            pltpu.VMEM((heads, rows), F32),
            pltpu.VMEM((heads, rows), F32),
            pltpu.VMEM((heads, rows, BLK), F32),
            pltpu.VMEM((heads, rows, BLK), F32),
            pltpu.VMEM((2, rows, BLK), F32),
            header,
            header,
            header,
            header,
            header,
            pltpu.VMEM((6, heads, dk), F32),
            sems,
            sems,
            sems,
            sems,
            sems,
            pltpu.SemaphoreType.DMA((5,)),
        ],
        compiler_params=pltpu.CompilerParams(
            collective_id=0, has_side_effects=True, vmem_limit_bytes=48 * 1024 * 1024
        ),
    )(*args)


def solution(mesh):
    rows = ("grp", "ctx", "head")
    placed = tuple(P(rows, *([None] * (n - 1))) for n in (2, 2, 2, 3, 2, 2, 2, 2, 2))
    return jax.shard_map(
        functools.partial(body, mesh.shape["ctx"], mesh.shape["head"]),
        mesh=mesh, in_specs=placed, out_specs=P(rows, None), check_vma=False,
    )
```

time: 250 us -> 108 us (0.43); the launches traced: 246 us -> 108 us
  Pallas kernels: 0 us -> 99.4 us
  waiting for transfers between devices: 73.4 us -> 0 us
  blocking collectives: 64.7 us -> 0 us
  other arithmetic: 41.4 us -> 0 us
  starting transfers between devices: 21.9 us -> 0 us
  between operations: 14.4 us -> 0.02 us
  matrix products: 12.9 us -> 0 us
  local copies, waits for them, and re-layouts: 17.6 us -> 8.1 us
    pallas_call x0 -> x1, Pallas kernels: none -> 99.4 us  [body(): pl.pallas_call(functools.partial(kernel, (heads, dk, dv, nc, nz)), out_sh...]
    all_to_all x5 -> x0, waiting for transfers between devices: 59.1 us -> none  [the longest x1 42.5 us: body(): lax.all_to_all(values, 'head', split_axis=1, concat_axis=0, tiled=True)]
    all_to_all x1 -> x0, blocking collectives: 53.2 us -> none  [body(): lax.all_to_all(hidden, 'head', split_axis=0, concat_axis=1, tiled=True)]
    all_to_all x5 -> x0, starting transfers between devices: 21.8 us -> none  [the longest x1 5.09 us: body(): lax.all_to_all(lookup_vectors, 'head', split_axis=1, concat_axis=0, tiled...]
    convert_element_type x6 -> x0, other arithmetic: 14.9 us -> none  [the longest x2 9.17 us: dequant(): return result.reshape(rows, heads, width).astype(jnp.bfloat16)]
    all_gather x1 -> x0, waiting for transfers between devices: 14.3 us -> none  [entering(): everything = jax.tree.map(lambda part: lax.all_gather(part, axis), x)]
    dot_general x5 -> x0, matrix products: 12.9 us -> none  [the longest x1 4.27 us: span_terms(): jnp.einsum('csgk,csgv->cgkv', weighted, values, preferred_element_type=jn...]
    select_n x14 -> x0, other arithmetic: 8.38 us -> none  [the longest x12 7.68 us: hop(): return jax.tree.map(lambda a, b: jnp.where(reached, a, b), new, before)]
  transfers between devices with their start and end apart: 6 -> 0, of which waited for: 4 -> 0; matrix products, arithmetic and copies ran while one was open for 14% -> 0% of each run, Pallas kernels for 0% -> 0%
where the time goes in v1:
time: 108 us
  Pallas kernels  99.4 us (92%)
  local copies, waits for them, and re-layouts  8.1 us (8%)
    pallas_call x1, Pallas kernels, body(): pl.pallas_call(functools.partial(kernel, (heads, dk, dv, nc, nz)), out_sh...  99.4 us
    unnamed x14, local copies, waits for them, and re-layouts  8.1 us

profile of v1, /device:TPU:2, one launch (start us, length us, event | category | flops | bytes accessed | tf_op | source)
XLA Modules:
  0.0 107.5 jit_solution(16727112270421250593)
XLA Ops:
  0.0 0.7 copy.10.scale_ref
  0.7 0.8 copy.11.ig_ref
  1.5 0.8 copy.12.fg_ref
  2.3 0.0 copy-start
  2.3 1.2 %copy-done = bf16[256,2048]{1,0:T(8,128)(2,1)S(1)} copy-done((bf16[256,2048]{1,0:T(8,128)(2,1)S(1)}, bf16[256,2048]{1,0:T(8,128)(2,1)}, u32[]{:S(2)}) %copy-start) | copy-done | bytes 1048600
  3.5 0.0 copy-start.1
  3.5 1.2 %copy-done.1 = bf16[256,2048]{1,0:T(8,128)(2,1)S(1)} copy-done((bf16[256,2048]{1,0:T(8,128)(2,1)S(1)}, bf16[256,2048]{1,0:T(8,128)(2,1)}, u32[]{:S(2)}) %copy-start.1) | copy-done | bytes 1048600
  4.8 0.0 copy-start.2
  4.8 0.7 copy-done.2
  5.4 0.0 copy-start.3
  5.4 0.7 copy-done.3
  6.1 0.0 copy-start.4
  6.1 0.7 copy-done.4
  6.8 99.4 %shard_map.91 = bf16[256,4096]{1,0:T(8,128)(2,1)S(1)} custom-call(bf16[256,2048]{1,0:T(8,128)(2,1)S(1)} %copy-done, bf16[256,2048]{1,0:T(8,128)(2,1)S(1)} %copy-done.1, bf16[256,4096]{1,0:T(8,128)(2,1)} %v_ref.1, f32[2,3,8]{2,1,0:T(4,128)S(1)} %copy.10.scale_ref, s32[2,8]{1,0:T(2,128)S(1)} %copy-done.2, s32[2,8]{1,0:T(2,128)S(1)} %copy-done.3, ...), custom_call_target="tpu_custom_call" | custom-call | tf_op jit(solution)/shard_map/pallas_call | solution.py:353
  106.2 1.3 %copy.14 = bf16[256,4096]{1,0:T(8,128)(2,1)} copy(bf16[256,4096]{1,0:T(8,128)(2,1)S(1)} %shard_map.91) | data formatting | bytes 4194304
Async XLA Ops:
  2.3 1.2 %copy-start = (bf16[256,2048]{1,0:T(8,128)(2,1)S(1)}, bf16[256,2048]{1,0:T(8,128)(2,1)}, u32[]{:S(2)}) copy-start(bf16[256,2048]{1,0:T(8,128)(2,1)} %q_ref.1) | copy-start | bytes 3145732
  3.5 1.2 %copy-start.1 = (bf16[256,2048]{1,0:T(8,128)(2,1)S(1)}, bf16[256,2048]{1,0:T(8,128)(2,1)}, u32[]{:S(2)}) copy-start(bf16[256,2048]{1,0:T(8,128)(2,1)} %k_ref.1) | copy-start | bytes 3145732
  4.8 0.7 copy-start.2
  5.4 0.7 copy-start.3
  6.1 0.7 copy-start.4

commit v2 on v1

--- a/solution.py
+++ b/solution.py
@@ -9,7 +9,9 @@
 from jax.sharding import PartitionSpec as P
 
 BLK = 128
-PIECES = 2
+PIECES = 4
+Z_SKEW = 6
+C_SKEW = 3
 NEG_FILL = -1e30
 MESH = pl.DeviceIdType.MESH
 F32 = jnp.float32
@@ -33,6 +35,7 @@
     vd,
     wk,
     num,
+    state,
     lifted,
     up_buf,
     tot_buf,
@@ -209,32 +212,43 @@
         wide = (slice(None), pl.ds(pl.multiple_of(h * dv, dv), dv))
         num[wide] = jnp.dot(product.astype(BF16), vd[wide], preferred_element_type=F32)
 
+    def head_state(h):
+        wide = (slice(None), pl.ds(pl.multiple_of(h * dv, dv), dv))
+        found = lax.dot_general(
+            wk[:, pl.ds(pl.multiple_of(h * dk, dk), dk)], vd[wide],
+            (((0,), (0,)), ((), ())), preferred_element_type=F32,
+        )
+        for p in range(PIECES):
+            state[p] = found[:, p * pw : (p + 1) * pw]
+
     def upward(i):
         h = lax.div(i, PIECES)
 
-        @pl.when(lax.rem(i, PIECES) == 0)
-        def _():
-            dequant(v_ref, 2, h, dv, vd)
-
-        piece = pl.ds(pl.multiple_of(i * pw, pw), pw)
-        state = lax.dot_general(
-            wk[:, pl.ds(pl.multiple_of(h * dk, dk), dk)], vd[:, piece],
-            (((0,), (0,)), ((), ())), preferred_element_type=F32,
-        )
-
         @pl.when(has_down)
         def _():
             up_copy(i).wait_recv()
 
-        tot_buf[i] = (weight(0, h) * up_buf[i].astype(F32) + weight(1, h) * state).astype(BF16)
+        mine = state[lax.rem(i, PIECES)]
+        tot_buf[i] = (weight(0, h) * up_buf[i].astype(F32) + weight(1, h) * mine).astype(BF16)
 
         @pl.when(has_up)
         def _():
             up_copy(i).start()
 
-        @pl.when(lax.rem(i, PIECES) == 0)
+    def ahead(i):
+        h, p = lax.div(i, PIECES), lax.rem(i, PIECES)
+
+        @pl.when(p == 0)
         def _():
             local(h)
+
+        @pl.when((p == PIECES - 2) & (h + 1 < heads))
+        def _():
+            dequant(v_ref, 2, h + 1, dv, vd)
+
+        @pl.when((p == PIECES - 1) & (h + 1 < heads))
+        def _():
+            head_state(h + 1)
 
     def header_row():
         @pl.when(has_row)
@@ -252,27 +266,30 @@
 
         join(r_h, up_h, own_h, 4)
 
+    def forward(j):
+        h = lax.div(j, PIECES)
+
+        @pl.when(j == 0)
+        def _():
+            header_row()
+
+        @pl.when(has_row)
+        def _():
+            down_copy(j).wait_recv()
+
+        @pl.when(has_row & has_down)
+        def _():
+            down_copy(j).start()
+
+        @pl.when(gives_row)
+        def _():
+            rs_buf[j] = (
+                weight(2, h) * r_buf[j].astype(F32) + weight(3, h) * tot_buf[j].astype(F32)
+            ).astype(BF16)
+            row_copy(j).start()
+
     def finish(j):
         h = lax.div(j, PIECES)
-
-        @pl.when(j == 0)
-        def _():
-            header_row()
-
-        @pl.when(has_row)
-        def _():
-            down_copy(j).wait_recv()
-
-        @pl.when(has_row & has_down)
-        def _():
-            down_copy(j).start()
-
-        arrived = r_buf[j].astype(F32)
-
-        @pl.when(gives_row)
-        def _():
-            rs_buf[j] = (weight(2, h) * arrived + weight(3, h) * tot_buf[j].astype(F32)).astype(BF16)
-            row_copy(j).start()
 
         @pl.when(lax.rem(j, PIECES) == 0)
         def _():
@@ -290,18 +307,28 @@
             fin[1] = 1.0 / jnp.maximum(jnp.abs(den), 1.0)
 
         piece = pl.ds(pl.multiple_of(j * pw, pw), pw)
-        begin = (weight(4, h) * arrived + weight(5, h) * up_buf[j].astype(F32)).astype(BF16)
+        begin = (weight(4, h) * r_buf[j].astype(F32) + weight(5, h) * up_buf[j].astype(F32)).astype(BF16)
         above_line = num[:, piece] * fin[0][:, 0:1] + jnp.dot(
             lifted[...], begin, preferred_element_type=F32
         )
         out_ref[:, piece] = (above_line * fin[1][:, 0:1]).astype(BF16)
 
-    skew = 2 * (last - z) + c
+    skew = Z_SKEW * (last - z) + C_SKEW * c
+    dequant(v_ref, 2, 0, dv, vd)
+    head_state(0)
 
     def step(t, carry):
         @pl.when(t < pieces)
         def _():
             upward(t)
+
+        @pl.when(t >= skew)
+        def _():
+            forward(t - skew)
+
+        @pl.when(t < pieces)
+        def _():
+            ahead(t)
 
         @pl.when(t >= skew)
         def _():
@@ -361,6 +388,7 @@
             pltpu.VMEM((rows, heads * dv), BF16),
             pltpu.VMEM((rows, heads * dk), BF16),
             pltpu.VMEM((rows, heads * dv), F32),
+            pltpu.VMEM((PIECES, dk, pw), F32),
             pltpu.VMEM((rows, dk), BF16),
             passed,
             passed,

time: 108 us -> 92.4 us (0.86)
  Pallas kernels: 99.4 us -> 82.8 us
    pallas_call x1, Pallas kernels: 99.4 us -> 82.8 us  [body(): pl.pallas_call(functools.partial(kernel, (heads, dk, dv, nc, nz)), out_sh...]
where the time goes in v2:
time: 92.4 us; the launch traced here: 91 us
  Pallas kernels  82.8 us (90%)
  local copies, waits for them, and re-layouts  8.1 us (9%)
    pallas_call x1, Pallas kernels, body(): pl.pallas_call(functools.partial(kernel, (heads, dk, dv, nc, nz)), out_sh...  82.8 us
    unnamed x14, local copies, waits for them, and re-layouts  8.1 us

profile of v2, /device:TPU:2, one launch (start us, length us, event | category | flops | bytes accessed | tf_op | source)
XLA Modules:
  0.0 91.0 jit_solution(11593732883033043158)
XLA Ops:
  0.0 0.7 copy.10.scale_ref
  0.7 0.8 copy.11.ig_ref
  1.5 0.8 copy.12.fg_ref
  2.3 0.0 copy-start
  2.3 1.2 %copy-done = bf16[256,2048]{1,0:T(8,128)(2,1)S(1)} copy-done((bf16[256,2048]{1,0:T(8,128)(2,1)S(1)}, bf16[256,2048]{1,0:T(8,128)(2,1)}, u32[]{:S(2)}) %copy-start) | copy-done | bytes 1048600
  3.5 0.0 copy-start.1
  3.5 1.2 %copy-done.1 = bf16[256,2048]{1,0:T(8,128)(2,1)S(1)} copy-done((bf16[256,2048]{1,0:T(8,128)(2,1)S(1)}, bf16[256,2048]{1,0:T(8,128)(2,1)}, u32[]{:S(2)}) %copy-start.1) | copy-done | bytes 1048600
  4.8 0.0 copy-start.2
  4.8 0.7 copy-done.2
  5.4 0.0 copy-start.3
  5.4 0.7 copy-done.3
  6.1 0.0 copy-start.4
  6.1 0.7 copy-done.4
  6.8 82.8 %shard_map.91 = bf16[256,4096]{1,0:T(8,128)(2,1)S(1)} custom-call(bf16[256,2048]{1,0:T(8,128)(2,1)S(1)} %copy-done, bf16[256,2048]{1,0:T(8,128)(2,1)S(1)} %copy-done.1, bf16[256,4096]{1,0:T(8,128)(2,1)} %v_ref.1, f32[2,3,8]{2,1,0:T(4,128)S(1)} %copy.10.scale_ref, s32[2,8]{1,0:T(2,128)S(1)} %copy-done.2, s32[2,8]{1,0:T(2,128)S(1)} %copy-done.3, ...), custom_call_target="tpu_custom_call" | custom-call | tf_op jit(solution)/shard_map/pallas_call | solution.py:380
  89.6 1.3 %copy.14 = bf16[256,4096]{1,0:T(8,128)(2,1)} copy(bf16[256,4096]{1,0:T(8,128)(2,1)S(1)} %shard_map.91) | data formatting | bytes 4194304
Async XLA Ops:
  2.3 1.2 %copy-start = (bf16[256,2048]{1,0:T(8,128)(2,1)S(1)}, bf16[256,2048]{1,0:T(8,128)(2,1)}, u32[]{:S(2)}) copy-start(bf16[256,2048]{1,0:T(8,128)(2,1)} %q_ref.1) | copy-start | bytes 3145732
  3.5 1.2 %copy-start.1 = (bf16[256,2048]{1,0:T(8,128)(2,1)S(1)}, bf16[256,2048]{1,0:T(8,128)(2,1)}, u32[]{:S(2)}) copy-start(bf16[256,2048]{1,0:T(8,128)(2,1)} %k_ref.1) | copy-start | bytes 3145732
  4.8 0.7 copy-start.2
  5.4 0.7 copy-start.3
  6.1 0.7 copy-start.4

commit v3 on v2

--- a/solution.py
+++ b/solution.py
@@ -10,8 +10,8 @@
 
 BLK = 128
 PIECES = 4
-Z_SKEW = 6
-C_SKEW = 3
+Z_SKEW = 3
+C_SKEW = 2
 NEG_FILL = -1e30
 MESH = pl.DeviceIdType.MESH
 F32 = jnp.float32
@@ -20,16 +20,22 @@
 
 def kernel(
     sizes,
-    q_ref,
-    k_ref,
-    v_ref,
+    q_any,
+    k_any,
+    v_any,
     scale_ref,
     ft_ref,
     fo_ref,
     fb_ref,
     ig_ref,
     fg_ref,
+    out_any,
     out_ref,
+    out_s,
+    q_ref,
+    k_ref,
+    v_ref,
+    in_s,
     qd,
     kd,
     vd,
@@ -37,6 +43,7 @@
     num,
     state,
     lifted,
+    inner,
     up_buf,
     tot_buf,
     r_buf,
@@ -63,6 +70,12 @@
 ):
     heads, dk, dv, nc, nz = sizes
     rows = q_ref.shape[0]
+    k_in = pltpu.make_async_copy(k_any, k_ref, in_s.at[0])
+    v_in = pltpu.make_async_copy(v_any, v_ref, in_s.at[1])
+    q_in = pltpu.make_async_copy(q_any, q_ref, in_s.at[2])
+    k_in.start()
+    v_in.start()
+    q_in.start()
     pw = dv // PIECES
     pieces = heads * PIECES
     factor = 1.0 / math.sqrt(dk)
@@ -117,7 +130,7 @@
             flip = jnp.where(ft_ref[b, h] == e, flip, 1.0)
             hit = lax.rem(lax.rem(off, dv), width)
             line = jnp.where(token == lax.div(off, dv), hit, -1)
-            scale = scale_ref[b, e, h]
+            scale = scale_ref[e, b, h]
             times = jnp.where(col == line, scale * flip, scale)
             kept[place] = (codes[place].astype(F32) * times).astype(BF16)
         return start
@@ -133,18 +146,20 @@
     logf = -(jnp.maximum(-forget, 0.0) + jnp.log1p(jnp.exp(-jnp.abs(forget))))
     gate = ig_ref[...].astype(F32)
     running = jnp.dot(
-        (line_t >= line_s).astype(F32), logf,
+        logf, (line_t <= line_s).astype(F32),
         preferred_element_type=F32, precision=lax.Precision.HIGHEST,
     )
-    bcol[...] = running
-    brow[...] = running.T
-    grow[...] = gate.T
-    exponent = running[rows - 1 : rows, :] - running + gate
-    wcol[...] = jnp.exp(exponent - jnp.max(exponent, axis=0, keepdims=True))
-    total = brow[:, rows - 1 : rows]
-    peak = jnp.max(total - brow[...] + grow[...], axis=1, keepdims=True)
+    brow[...] = running
+    bcol[...] = running.T
+    grow[...] = gate
+    total = running[:, rows - 1 : rows]
+    exponent = total - running + gate
+    peak = jnp.max(exponent, axis=1, keepdims=True)
+    wcol[...] = jnp.exp(exponent - peak).T
     own_h[:, dk : 2 * dk] = jnp.broadcast_to(peak, (heads, dk))
     own_h[:, 2 * dk :] = jnp.broadcast_to(total, (heads, dk))
+
+    k_in.wait()
 
     def keys(h, carry):
         start = dequant(k_ref, 1, h, dk, kd)
@@ -154,7 +169,7 @@
         own_h[pl.ds(h, 1), pl.ds(0, dk)] = jnp.sum(weighted.astype(F32), axis=0, keepdims=True)
         return carry
 
-    lax.fori_loop(0, heads, keys, 0)
+    lax.fori_loop(0, heads, keys, 0, unroll=2)
 
     def empty_header(ref):
         ref[:, 0:dk] = jnp.zeros((heads, dk), F32)
@@ -209,8 +224,11 @@
         product = jnp.exp(gaps - top) * scores
         peak_l[h] = jnp.broadcast_to(top, (rows, BLK))
         den_l[h] = jnp.broadcast_to(jnp.sum(product, axis=1, keepdims=True), (rows, BLK))
+        inner[...] = product.astype(BF16)
+
+    def local_values(h):
         wide = (slice(None), pl.ds(pl.multiple_of(h * dv, dv), dv))
-        num[wide] = jnp.dot(product.astype(BF16), vd[wide], preferred_element_type=F32)
+        num[wide] = jnp.dot(inner[...], vd[wide], preferred_element_type=F32)
 
     def head_state(h):
         wide = (slice(None), pl.ds(pl.multiple_of(h * dv, dv), dv))
@@ -241,6 +259,10 @@
         @pl.when(p == 0)
         def _():
             local(h)
+
+        @pl.when(p == min(1, PIECES - 1))
+        def _():
+            local_values(h)
 
         @pl.when((p == PIECES - 2) & (h + 1 < heads))
         def _():
@@ -313,16 +335,26 @@
         )
         out_ref[:, piece] = (above_line * fin[1][:, 0:1]).astype(BF16)
 
+        @pl.when(lax.rem(j, PIECES) == PIECES - 1)
+        def _():
+            out_copy(h).start()
+
+    def out_copy(h):
+        wide = (slice(None), pl.ds(pl.multiple_of(h * dv, dv), dv))
+        return pltpu.make_async_copy(out_ref.at[wide], out_any.at[wide], out_s.at[h])
+
     skew = Z_SKEW * (last - z) + C_SKEW * c
+    v_in.wait()
     dequant(v_ref, 2, 0, dv, vd)
     head_state(0)
+    q_in.wait()
 
     def step(t, carry):
         @pl.when(t < pieces)
         def _():
             upward(t)
 
-        @pl.when(t >= skew)
+        @pl.when((t >= skew) & (t < pieces + skew))
         def _():
             forward(t - skew)
 
@@ -330,13 +362,13 @@
         def _():
             ahead(t)
 
-        @pl.when(t >= skew)
-        def _():
-            finish(t - skew)
+        @pl.when(t > skew)
+        def _():
+            finish(t - skew - 1)
 
         return carry
 
-    lax.fori_loop(0, pieces + skew, step, 0)
+    lax.fori_loop(0, pieces + skew + 1, step, 0)
 
     @pl.when(has_up)
     def _():
@@ -349,6 +381,12 @@
     @pl.when(gives_row)
     def _():
         row_head.wait_send()
+
+    def drain_out(h, carry):
+        out_copy(h).wait()
+        return carry
+
+    lax.fori_loop(0, heads, drain_out, 0)
 
     def drain(i, carry):
         @pl.when(has_up)
@@ -380,9 +418,15 @@
     return pl.pallas_call(
         functools.partial(kernel, (heads, dk, dv, nc, nz)),
         out_shape=jax.ShapeDtypeStruct((rows, heads * dv), BF16),
-        in_specs=[vmem] * 3 + [smem] * 4 + [vmem] * 2,
-        out_specs=vmem,
+        in_specs=[pl.BlockSpec(memory_space=pl.ANY)] * 3 + [smem] * 4 + [vmem] * 2,
+        out_specs=pl.BlockSpec(memory_space=pl.ANY),
         scratch_shapes=[
+            pltpu.VMEM((rows, heads * dv), BF16),
+            pltpu.SemaphoreType.DMA((heads,)),
+            pltpu.VMEM((rows, heads * dk), BF16),
+            pltpu.VMEM((rows, heads * dk), BF16),
+            pltpu.VMEM((rows, heads * dv), BF16),
+            pltpu.SemaphoreType.DMA((3,)),
             pltpu.VMEM((rows, heads * dk), BF16),
             pltpu.VMEM((rows, heads * dk), BF16),
             pltpu.VMEM((rows, heads * dv), BF16),
@@ -390,6 +434,7 @@
             pltpu.VMEM((rows, heads * dv), F32),
             pltpu.VMEM((PIECES, dk, pw), F32),
             pltpu.VMEM((rows, dk), BF16),
+            pltpu.VMEM((rows, rows), BF16),
             passed,
             passed,
             passed,
@@ -415,9 +460,9 @@
             pltpu.SemaphoreType.DMA((5,)),
         ],
         compiler_params=pltpu.CompilerParams(
-            collective_id=0, has_side_effects=True, vmem_limit_bytes=48 * 1024 * 1024
+            collective_id=0, has_side_effects=True, vmem_limit_bytes=60 * 1024 * 1024
         ),
-    )(*args)
+    )(*args[:3], args[3].transpose(1, 0, 2), *args[4:7], args[7].T, args[8].T)
 
 
 def solution(mesh):

time: 92.4 us -> 102 us (1.10)
  Pallas kernels: 82.8 us -> 98.4 us
  local copies, waits for them, and re-layouts: 8.1 us -> 3.13 us
    pallas_call x1, Pallas kernels: 82.8 us -> 98.4 us  [body(): pl.pallas_call(functools.partial(kernel, (heads, dk, dv, nc, nz)), out_sh...]
    unnamed x14 -> x1, local copies, waits for them, and re-layouts: 8.1 us -> 3.13 us
where the time goes in v3:
time: 102 us
  Pallas kernels  98.4 us (96%)
  local copies, waits for them, and re-layouts  3.13 us (3%)
    pallas_call x1, Pallas kernels, body(): pl.pallas_call(functools.partial(kernel, (heads, dk, dv, nc, nz)), out_sh...  98.4 us
    unnamed x1, local copies, waits for them, and re-layouts  3.13 us

profile of v3, /device:TPU:2, one launch (start us, length us, event | category | flops | bytes accessed | tf_op | source)
XLA Modules:
  0.0 101.5 jit_solution(14146993155103013618)
XLA Ops:
  0.0 98.4 %shard_map.91 = bf16[256,4096]{1,0:T(8,128)(2,1)} custom-call(bf16[256,2048]{1,0:T(8,128)(2,1)} %q_any.1, bf16[256,2048]{1,0:T(8,128)(2,1)} %k_any.1, bf16[256,4096]{1,0:T(8,128)(2,1)} %v_any.1, f32[3,2,8]{2,1,0:T(2,128)} %bitcast.5, s32[2,8]{1,0:T(2,128)} %ft_ref.1, s32[2,8]{1,0:T(2,128)} %fo_ref.1, s32[2,8]{1,0:T(2,128)} %fb_ref.1, ...), custom_call_target="tpu_custom_call" | custom-call | tf_op jit(solution)/shard_map/pallas_call | solution.py:418
  98.4 3.1 %copy.11 = bf16[256,4096]{1,0:T(8,128)(2,1)} copy(bf16[256,4096]{1,0:T(8,128)(2,1)} %shard_map.91) | data formatting | bytes 4194304

commit v4 on v3

--- a/solution.py
+++ b/solution.py
@@ -10,8 +10,6 @@
 
 BLK = 128
 PIECES = 4
-Z_SKEW = 3
-C_SKEW = 2
 NEG_FILL = -1e30
 MESH = pl.DeviceIdType.MESH
 F32 = jnp.float32
@@ -46,8 +44,6 @@
     inner,
     up_buf,
     tot_buf,
-    r_buf,
-    rs_buf,
     bcol,
     wcol,
     brow,
@@ -58,14 +54,9 @@
     own_h,
     up_h,
     tot_h,
-    r_h,
-    rs_h,
     wts,
     up_s,
     up_r,
-    dn_s,
-    r_r,
-    cx_s,
     hs,
 ):
     heads, dk, dv, nc, nz = sizes
@@ -80,17 +71,14 @@
     pieces = heads * PIECES
     factor = 1.0 / math.sqrt(dk)
     g, c, z = lax.axis_index("grp"), lax.axis_index("ctx"), lax.axis_index("head")
-    last = nz - 1
-    has_up, has_down = z < last, z > 0
-    at_end = z == last
-    gives_row, has_row = at_end & (c < nc - 1), c > 0
-    above = (g, c, jnp.minimum(z + 1, last))
-    below = (g, c, jnp.maximum(z - 1, 0))
-    after = (g, jnp.minimum(c + 1, nc - 1), z)
-    earlier = (g, jnp.maximum(c - 1, 0), z)
+    place = c * nz + z
+    has_up, has_down = place < nc * nz - 1, place > 0
+    onward, prior = jnp.minimum(place + 1, nc * nz - 1), jnp.maximum(place - 1, 0)
+    above = (g, lax.div(onward, nz), lax.rem(onward, nz))
+    below = (g, lax.div(prior, nz), lax.rem(prior, nz))
 
     barrier = pltpu.get_barrier_semaphore()
-    greet = ((has_up, above), (has_down, below), (gives_row, after), (at_end & has_row, earlier))
+    greet = ((has_up, above), (has_down, below))
     for there, who in greet:
 
         @pl.when(there)
@@ -106,15 +94,7 @@
     def up_copy(i):
         return remote(tot_buf.at[i], up_buf.at[i], up_s.at[i], up_r.at[i], above)
 
-    def down_copy(i):
-        return remote(r_buf.at[i], r_buf.at[i], dn_s.at[i], r_r.at[i], below)
-
-    def row_copy(i):
-        return remote(rs_buf.at[i], r_buf.at[i], cx_s.at[i], r_r.at[i], after)
-
     up_head = remote(tot_h, up_h, hs.at[0], hs.at[1], above)
-    down_head = remote(r_h, r_h, hs.at[2], hs.at[3], below)
-    row_head = remote(rs_h, r_h, hs.at[4], hs.at[3], after)
 
     token = lax.broadcasted_iota(jnp.int32, (BLK, 1), 0)
 
@@ -176,15 +156,10 @@
         ref[:, dk : 2 * dk] = jnp.full((heads, dk), NEG_FILL, F32)
         ref[:, 2 * dk :] = jnp.zeros((heads, dk), F32)
 
-    @pl.when(z == 0)
+    @pl.when(place == 0)
     def _():
         empty_header(up_h)
         up_buf[...] = jnp.zeros_like(up_buf)
-
-    @pl.when(c == 0)
-    def _():
-        empty_header(r_h)
-        r_buf[...] = jnp.zeros_like(r_buf)
 
     def join(first, later, dst, at):
         m1, m2, f2 = first[:, dk : 2 * dk], later[:, dk : 2 * dk], later[:, 2 * dk :]
@@ -195,19 +170,6 @@
         dst[:, 0:dk] = w1 * first[:, 0:dk] + w2 * later[:, 0:dk]
         dst[:, dk : 2 * dk] = m
         dst[:, 2 * dk :] = first[:, 2 * dk :] + f2
-
-    greeted = sum(there.astype(jnp.int32) for there, _ in greet)
-    pl.semaphore_wait(barrier, greeted)
-
-    @pl.when(has_down)
-    def _():
-        up_head.wait_recv()
-
-    join(up_h, own_h, tot_h, 0)
-
-    @pl.when(has_up)
-    def _():
-        up_head.start()
 
     def weight(at, h):
         return wts[at, pl.ds(h, 1), :][:, 0:pw]
@@ -237,7 +199,7 @@
             (((0,), (0,)), ((), ())), preferred_element_type=F32,
         )
         for p in range(PIECES):
-            state[p] = found[:, p * pw : (p + 1) * pw]
+            state[h * PIECES + p] = found[:, p * pw : (p + 1) * pw]
 
     def upward(i):
         h = lax.div(i, PIECES)
@@ -246,69 +208,38 @@
         def _():
             up_copy(i).wait_recv()
 
-        mine = state[lax.rem(i, PIECES)]
+        mine = state[i]
         tot_buf[i] = (weight(0, h) * up_buf[i].astype(F32) + weight(1, h) * mine).astype(BF16)
 
         @pl.when(has_up)
         def _():
             up_copy(i).start()
 
-    def ahead(i):
-        h, p = lax.div(i, PIECES), lax.rem(i, PIECES)
-
-        @pl.when(p == 0)
+    def ready(h, carry):
+        dequant(v_ref, 2, h, dv, vd)
+        head_state(h)
+        local(h)
+        local_values(h)
+        return carry
+
+    def ahead(i, done):
+        h, p = lax.div(i, PIECES) + done, lax.rem(i, PIECES)
+
+        @pl.when((p == 0) & (h < heads))
+        def _():
+            dequant(v_ref, 2, h, dv, vd)
+
+        @pl.when((p == min(1, PIECES - 1)) & (h < heads))
+        def _():
+            head_state(h)
+
+        @pl.when((p == max(0, PIECES - 2)) & (h < heads))
         def _():
             local(h)
 
-        @pl.when(p == min(1, PIECES - 1))
+        @pl.when((p == PIECES - 1) & (h < heads))
         def _():
             local_values(h)
-
-        @pl.when((p == PIECES - 2) & (h + 1 < heads))
-        def _():
-            dequant(v_ref, 2, h + 1, dv, vd)
-
-        @pl.when((p == PIECES - 1) & (h + 1 < heads))
-        def _():
-            head_state(h + 1)
-
-    def header_row():
-        @pl.when(has_row)
-        def _():
-            down_head.wait_recv()
-
-        @pl.when(has_row & has_down)
-        def _():
-            down_head.start()
-
-        @pl.when(gives_row)
-        def _():
-            join(r_h, tot_h, rs_h, 2)
-            row_head.start()
-
-        join(r_h, up_h, own_h, 4)
-
-    def forward(j):
-        h = lax.div(j, PIECES)
-
-        @pl.when(j == 0)
-        def _():
-            header_row()
-
-        @pl.when(has_row)
-        def _():
-            down_copy(j).wait_recv()
-
-        @pl.when(has_row & has_down)
-        def _():
-            down_copy(j).start()
-
-        @pl.when(gives_row)
-        def _():
-            rs_buf[j] = (
-                weight(2, h) * r_buf[j].astype(F32) + weight(3, h) * tot_buf[j].astype(F32)
-            ).astype(BF16)
-            row_copy(j).start()
 
     def finish(j):
         h = lax.div(j, PIECES)
@@ -316,7 +247,7 @@
         @pl.when(lax.rem(j, PIECES) == 0)
         def _():
             place = (slice(None), pl.ds(pl.multiple_of(h * dk, dk), dk))
-            header = own_h[pl.ds(h, 1), :]
+            header = up_h[pl.ds(h, 1), :]
             norm, m = header[:, 0:dk], header[:, dk : dk + BLK]
             inter = column(bcol, h) + m
             top = jnp.maximum(peak_l[h], inter)
@@ -329,9 +260,8 @@
             fin[1] = 1.0 / jnp.maximum(jnp.abs(den), 1.0)
 
         piece = pl.ds(pl.multiple_of(j * pw, pw), pw)
-        begin = (weight(4, h) * r_buf[j].astype(F32) + weight(5, h) * up_buf[j].astype(F32)).astype(BF16)
         above_line = num[:, piece] * fin[0][:, 0:1] + jnp.dot(
-            lifted[...], begin, preferred_element_type=F32
+            lifted[...], up_buf[j], preferred_element_type=F32
         )
         out_ref[:, piece] = (above_line * fin[1][:, 0:1]).astype(BF16)
 
@@ -343,45 +273,36 @@
         wide = (slice(None), pl.ds(pl.multiple_of(h * dv, dv), dv))
         return pltpu.make_async_copy(out_ref.at[wide], out_any.at[wide], out_s.at[h])
 
-    skew = Z_SKEW * (last - z) + C_SKEW * c
     v_in.wait()
-    dequant(v_ref, 2, 0, dv, vd)
-    head_state(0)
     q_in.wait()
+    done = jnp.minimum(heads, 1 + lax.div(3 * place, 4))
+    lax.fori_loop(0, done, ready, 0)
+
+    greeted = sum(there.astype(jnp.int32) for there, _ in greet)
+    pl.semaphore_wait(barrier, greeted)
+
+    @pl.when(has_down)
+    def _():
+        up_head.wait_recv()
+
+    join(up_h, own_h, tot_h, 0)
+
+    @pl.when(has_up)
+    def _():
+        up_head.start()
 
     def step(t, carry):
-        @pl.when(t < pieces)
-        def _():
-            upward(t)
-
-        @pl.when((t >= skew) & (t < pieces + skew))
-        def _():
-            forward(t - skew)
-
-        @pl.when(t < pieces)
-        def _():
-            ahead(t)
-
-        @pl.when(t > skew)
-        def _():
-            finish(t - skew - 1)
-
-        return carry
-
-    lax.fori_loop(0, pieces + skew + 1, step, 0)
+        upward(t)
+        ahead(t, done)
+        finish(t)
+        return carry
+
+    lax.fori_loop(0, pieces, step, 0)
 
     @pl.when(has_up)
     def _():
         up_head.wait_send()
 
-    @pl.when(has_row & has_down)
-    def _():
-        down_head.wait_send()
-
-    @pl.when(gives_row)
-    def _():
-        row_head.wait_send()
-
     def drain_out(h, carry):
         out_copy(h).wait()
         return carry
@@ -392,14 +313,6 @@
         @pl.when(has_up)
         def _():
             up_copy(i).wait_send()
-
-        @pl.when(has_row & has_down)
-        def _():
-            down_copy(i).wait_send()
-
-        @pl.when(gives_row)
-        def _():
-            row_copy(i).wait_send()
 
         return carry
 
@@ -432,11 +345,9 @@
             pltpu.VMEM((rows, heads * dv), BF16),
             pltpu.VMEM((rows, heads * dk), BF16),
             pltpu.VMEM((rows, heads * dv), F32),
-            pltpu.VMEM((PIECES, dk, pw), F32),
+            pltpu.VMEM((pieces, dk, pw), F32),
             pltpu.VMEM((rows, dk), BF16),
             pltpu.VMEM((rows, rows), BF16),
-            passed,
-            passed,
             passed,
             passed,
             pltpu.VMEM((rows, heads), F32),
@@ -449,15 +360,10 @@
             header,
             header,
             header,
-            header,
-            header,
-            pltpu.VMEM((6, heads, dk), F32),
+            pltpu.VMEM((2, heads, dk), F32),
             sems,
             sems,
-            sems,
-            sems,
-            sems,
-            pltpu.SemaphoreType.DMA((5,)),
+            pltpu.SemaphoreType.DMA((2,)),
         ],
         compiler_params=pltpu.CompilerParams(
             collective_id=0, has_side_effects=True, vmem_limit_bytes=60 * 1024 * 1024

time: 102 us -> 100 us (0.980)
  the two profiles are of different devices: /device:TPU:2 before, /device:TPU:31 now
where the time goes in v4:
time: 100 us
  Pallas kernels  97.1 us (97%)
  local copies, waits for them, and re-layouts  3.13 us (3%)
    pallas_call x1, Pallas kernels, body(): pl.pallas_call(functools.partial(kernel, (heads, dk, dv, nc, nz)), out_sh...  97.1 us
    unnamed x1, local copies, waits for them, and re-layouts  3.13 us

profile of v4, /device:TPU:31, one launch (start us, length us, event | category | flops | bytes accessed | tf_op | source)
XLA Modules:
  0.0 100.3 jit_solution(2319613815819980188)
XLA Ops:
  0.0 97.1 %shard_map.91 = bf16[256,4096]{1,0:T(8,128)(2,1)} custom-call(bf16[256,2048]{1,0:T(8,128)(2,1)} %q_any.1, bf16[256,2048]{1,0:T(8,128)(2,1)} %k_any.1, bf16[256,4096]{1,0:T(8,128)(2,1)} %v_any.1, f32[3,2,8]{2,1,0:T(2,128)} %bitcast.5, s32[2,8]{1,0:T(2,128)} %ft_ref.1, s32[2,8]{1,0:T(2,128)} %fo_ref.1, s32[2,8]{1,0:T(2,128)} %fb_ref.1, ...), custom_call_target="tpu_custom_call" | custom-call | tf_op jit(solution)/shard_map/pallas_call | solution.py:331
  97.1 3.1 %copy.11 = bf16[256,4096]{1,0:T(8,128)(2,1)} copy(bf16[256,4096]{1,0:T(8,128)(2,1)} %shard_map.91) | data formatting | bytes 4194304

commit v5 on v4

--- a/solution.py
+++ b/solution.py
@@ -215,9 +215,12 @@
         def _():
             up_copy(i).start()
 
-    def ready(h, carry):
+    def states(h, carry):
         dequant(v_ref, 2, h, dv, vd)
         head_state(h)
+        return carry
+
+    def locals_of(h, carry):
         local(h)
         local_values(h)
         return carry
@@ -232,14 +235,6 @@
         @pl.when((p == min(1, PIECES - 1)) & (h < heads))
         def _():
             head_state(h)
-
-        @pl.when((p == max(0, PIECES - 2)) & (h < heads))
-        def _():
-            local(h)
-
-        @pl.when((p == PIECES - 1) & (h < heads))
-        def _():
-            local_values(h)
 
     def finish(j):
         h = lax.div(j, PIECES)
@@ -275,8 +270,13 @@
 
     v_in.wait()
     q_in.wait()
-    done = jnp.minimum(heads, 1 + lax.div(3 * place, 4))
-    lax.fori_loop(0, done, ready, 0)
+    early = 2 * place < nc * nz
+    done = jnp.minimum(heads, 1 + jnp.where(early, place, heads))
+    lax.fori_loop(0, done, states, 0)
+
+    @pl.when(jnp.logical_not(early))
+    def _():
+        lax.fori_loop(0, heads, locals_of, 0)
 
     greeted = sum(there.astype(jnp.int32) for there, _ in greet)
     pl.semaphore_wait(barrier, greeted)
@@ -293,11 +293,28 @@
 
     def step(t, carry):
         upward(t)
-        ahead(t, done)
-        finish(t)
+
+        @pl.when(early)
+        def _():
+            ahead(t, done)
+
+        @pl.when(jnp.logical_not(early))
+        def _():
+            finish(t)
+
         return carry
 
     lax.fori_loop(0, pieces, step, 0)
+
+    @pl.when(early)
+    def _():
+        lax.fori_loop(0, heads, locals_of, 0)
+
+        def rest(t, carry):
+            finish(t)
+            return carry
+
+        lax.fori_loop(0, pieces, rest, 0)
 
     @pl.when(has_up)
     def _():

time: 100 us -> 100 us (level)
  no operation moved by 1% of the time
where the time goes in v5:
time: 100 us
  Pallas kernels  96.9 us (97%)
  local copies, waits for them, and re-layouts  3.13 us (3%)
    pallas_call x1, Pallas kernels, body(): pl.pallas_call(functools.partial(kernel, (heads, dk, dv, nc, nz)), out_sh...  96.9 us
    unnamed x1, local copies, waits for them, and re-layouts  3.13 us

profile of v5, /device:TPU:31, one launch (start us, length us, event | category | flops | bytes accessed | tf_op | source)
XLA Modules:
  0.0 100.0 jit_solution(9402022975413610341)
XLA Ops:
  0.0 96.9 %shard_map.91 = bf16[256,4096]{1,0:T(8,128)(2,1)} custom-call(bf16[256,2048]{1,0:T(8,128)(2,1)} %q_any.1, bf16[256,2048]{1,0:T(8,128)(2,1)} %k_any.1, bf16[256,4096]{1,0:T(8,128)(2,1)} %v_any.1, f32[3,2,8]{2,1,0:T(2,128)} %bitcast.5, s32[2,8]{1,0:T(2,128)} %ft_ref.1, s32[2,8]{1,0:T(2,128)} %fo_ref.1, s32[2,8]{1,0:T(2,128)} %fb_ref.1, ...), custom_call_target="tpu_custom_call" | custom-call | tf_op jit(solution)/shard_map/pallas_call | solution.py:348
  96.9 3.1 %copy.11 = bf16[256,4096]{1,0:T(8,128)(2,1)} copy(bf16[256,4096]{1,0:T(8,128)(2,1)} %shard_map.91) | data formatting | bytes 4194304

commit v6 on v5

--- a/solution.py
+++ b/solution.py
@@ -44,6 +44,7 @@
     inner,
     up_buf,
     tot_buf,
+    relay,
     bcol,
     wcol,
     brow,
@@ -57,6 +58,8 @@
     wts,
     up_s,
     up_r,
+    rl_s,
+    rl_r,
     hs,
 ):
     heads, dk, dv, nc, nz = sizes
@@ -78,7 +81,16 @@
     below = (g, lax.div(prior, nz), lax.rem(prior, nz))
 
     barrier = pltpu.get_barrier_semaphore()
-    greet = ((has_up, above), (has_down, below))
+    mid = nc * nz // 2 - 1
+    first = (g, 0, 0)
+    half = (g, mid // nz, mid % nz)
+    over = (g, (mid + 1) // nz, (mid + 1) % nz)
+    is_first, is_half, is_over = place == 0, place == mid, place == mid + 1
+    direct = has_up & (place != mid)
+    greet = (
+        (has_up, above), (has_down, below), (is_half, first), (is_over, first),
+        (is_first, half), (is_first, over),
+    )
     for there, who in greet:
 
         @pl.when(there)
@@ -93,6 +105,12 @@
 
     def up_copy(i):
         return remote(tot_buf.at[i], up_buf.at[i], up_s.at[i], up_r.at[i], above)
+
+    def relay_copy(i):
+        return remote(tot_buf.at[i], relay.at[i], up_s.at[i], rl_r.at[i], first)
+
+    def relay_on(i):
+        return remote(relay.at[i], up_buf.at[i], rl_s.at[i], up_r.at[i], over)
 
     up_head = remote(tot_h, up_h, hs.at[0], hs.at[1], above)
 
@@ -211,9 +229,13 @@
         mine = state[i]
         tot_buf[i] = (weight(0, h) * up_buf[i].astype(F32) + weight(1, h) * mine).astype(BF16)
 
-        @pl.when(has_up)
+        @pl.when(direct)
         def _():
             up_copy(i).start()
+
+        @pl.when(is_half)
+        def _():
+            relay_copy(i).start()
 
     def states(h, carry):
         dequant(v_ref, 2, h, dv, vd)
@@ -306,6 +328,15 @@
 
     lax.fori_loop(0, pieces, step, 0)
 
+    @pl.when(is_first)
+    def _():
+        def pass_on(i, carry):
+            relay_copy(i).wait_recv()
+            relay_on(i).start()
+            return carry
+
+        lax.fori_loop(0, pieces, pass_on, 0)
+
     @pl.when(early)
     def _():
         lax.fori_loop(0, heads, locals_of, 0)
@@ -327,9 +358,17 @@
     lax.fori_loop(0, heads, drain_out, 0)
 
     def drain(i, carry):
-        @pl.when(has_up)
+        @pl.when(direct)
         def _():
             up_copy(i).wait_send()
+
+        @pl.when(is_half)
+        def _():
+            relay_copy(i).wait_send()
+
+        @pl.when(is_first)
+        def _():
+            relay_on(i).wait_send()
 
         return carry
 
@@ -367,6 +406,7 @@
             pltpu.VMEM((rows, rows), BF16),
             passed,
             passed,
+            passed,
             pltpu.VMEM((rows, heads), F32),
             pltpu.VMEM((rows, heads), F32),
             pltpu.VMEM((heads, rows), F32),
@@ -380,6 +420,8 @@
             pltpu.VMEM((2, heads, dk), F32),
             sems,
             sems,
+            sems,
+            sems,
             pltpu.SemaphoreType.DMA((2,)),
         ],
         compiler_params=pltpu.CompilerParams(

time: 100 us -> 103 us (1.030)
  the two profiles are of different devices: /device:TPU:31 before, /device:TPU:27 now
where the time goes in v6:
time: 103 us
  Pallas kernels  99.8 us (97%)
  local copies, waits for them, and re-layouts  3.13 us (3%)
    pallas_call x1, Pallas kernels, body(): pl.pallas_call(functools.partial(kernel, (heads, dk, dv, nc, nz)), out_sh...  99.8 us
    unnamed x1, local copies, waits for them, and re-layouts  3.13 us

profile of v6, /device:TPU:27, one launch (start us, length us, event | category | flops | bytes accessed | tf_op | source)
XLA Modules:
  0.0 102.9 jit_solution(18329532079674899726)
XLA Ops:
  0.0 99.8 %shard_map.91 = bf16[256,4096]{1,0:T(8,128)(2,1)} custom-call(bf16[256,2048]{1,0:T(8,128)(2,1)} %q_any.1, bf16[256,2048]{1,0:T(8,128)(2,1)} %k_any.1, bf16[256,4096]{1,0:T(8,128)(2,1)} %v_any.1, f32[3,2,8]{2,1,0:T(2,128)} %bitcast.5, s32[2,8]{1,0:T(2,128)} %ft_ref.1, s32[2,8]{1,0:T(2,128)} %fo_ref.1, s32[2,8]{1,0:T(2,128)} %fb_ref.1, ...), custom_call_target="tpu_custom_call" | custom-call | tf_op jit(solution)/shard_map/pallas_call | solution.py:387
  99.8 3.1 %copy.11 = bf16[256,4096]{1,0:T(8,128)(2,1)} copy(bf16[256,4096]{1,0:T(8,128)(2,1)} %shard_map.91) | data formatting | bytes 4194304

commit v7 on v3

--- a/solution.py
+++ b/solution.py
@@ -10,8 +10,8 @@
 
 BLK = 128
 PIECES = 4
-Z_SKEW = 3
-C_SKEW = 2
+Z_SKEW = 5
+C_SKEW = 3
 NEG_FILL = -1e30
 MESH = pl.DeviceIdType.MESH
 F32 = jnp.float32

time: 102 us -> 85.8 us (0.84)
  Pallas kernels: 98.4 us -> 82.5 us
    pallas_call x1, Pallas kernels: 98.4 us -> 82.5 us  [body(): pl.pallas_call(functools.partial(kernel, (heads, dk, dv, nc, nz)), out_sh...]
where the time goes in v7:
time: 85.8 us; the launch traced here: 85.6 us
  Pallas kernels  82.5 us (96%)
  local copies, waits for them, and re-layouts  3.13 us (4%)
    pallas_call x1, Pallas kernels, body(): pl.pallas_call(functools.partial(kernel, (heads, dk, dv, nc, nz)), out_sh...  82.5 us
    unnamed x1, local copies, waits for them, and re-layouts  3.13 us

profile of v7, /device:TPU:2, one launch (start us, length us, event | category | flops | bytes accessed | tf_op | source)
XLA Modules:
  0.0 85.6 jit_solution(18061426848858558540)
XLA Ops:
  0.0 82.5 %shard_map.91 = bf16[256,4096]{1,0:T(8,128)(2,1)} custom-call(bf16[256,2048]{1,0:T(8,128)(2,1)} %q_any.1, bf16[256,2048]{1,0:T(8,128)(2,1)} %k_any.1, bf16[256,4096]{1,0:T(8,128)(2,1)} %v_any.1, f32[3,2,8]{2,1,0:T(2,128)} %bitcast.5, s32[2,8]{1,0:T(2,128)} %ft_ref.1, s32[2,8]{1,0:T(2,128)} %fo_ref.1, s32[2,8]{1,0:T(2,128)} %fb_ref.1, ...), custom_call_target="tpu_custom_call" | custom-call | tf_op jit(solution)/shard_map/pallas_call | solution.py:418
  82.5 3.1 %copy.11 = bf16[256,4096]{1,0:T(8,128)(2,1)} copy(bf16[256,4096]{1,0:T(8,128)(2,1)} %shard_map.91) | data formatting | bytes 4194304
